TPU v7x, 512 devices: a whole 4x4x16 slice. The times are simulated.
512 devices in a mesh: fsdp: 32 (over z, x_hi), tensor: 16 (over x_lo, y, core).
Axes of the slice: x: 4 (x_hi: 2, x_lo: 2; x = x_hi * 2 + x_lo), y: 4, z: 16, core: 2. Of those that a mesh axis runs over, the one named last changes fastest.
Arguments:
- grad_out: bfloat16 [512, 16384], P('fsdp', 'tensor'), may hold values from -1.1953125 to 1.1953125
- gate_pre: bfloat16 [512, 26624], P('fsdp', 'tensor'), may hold values from -6 to 6
- up_pre: bfloat16 [512, 26624], P('fsdp', 'tensor'), may hold values from -6 to 6
- down_weight: bfloat16 [26624, 16384], P('tensor', 'fsdp'), may hold values from -0.0390625 to 0.0390625
Outputs:
- grad_gate: bfloat16 [512, 26624], P('fsdp', 'tensor')
- grad_up: bfloat16 [512, 26624], P('fsdp', 'tensor')
- grad_weight: bfloat16 [26624, 16384], P('tensor', 'fsdp')
All inputs are finite; a program needn't handle non-finite values.
Results may differ from a plain program's by a relative error of at most 0.0049.
Values may be sent and summed in bfloat16 or wider, within the bound.
A program may use at most 64 MiB of HBM per device.

v0:
```python
import jax
import jax.numpy as jnp
from jax import lax
from jax.sharding import PartitionSpec as P


def shards(grad_out, gate_pre, up_pre, down_weight):
    full_rows = lax.all_gather(grad_out, "tensor", axis=1, tiled=True)
    spread = lax.all_to_all(full_rows, "fsdp", split_axis=1, concat_axis=0, tiled=True)
    group_rows = gate_pre.shape[0]
    gate = gate_pre.astype(jnp.float32)
    up = up_pre.astype(jnp.float32)
    hidden = (jax.nn.silu(gate) * up).astype(jnp.bfloat16)
    contract = (((1,), (1,)), ((), ()))
    partial_all = lax.dot_general(spread, down_weight, contract, preferred_element_type=jnp.float32)
    summed = lax.psum(partial_all, "fsdp")
    position = lax.axis_index("fsdp") * group_rows
    grad_hidden = lax.dynamic_slice_in_dim(summed, position, group_rows, 0)
    sig = jax.nn.sigmoid(gate)
    grad_gate = (grad_hidden * up * sig * (1.0 + gate * (1.0 - sig))).astype(jnp.bfloat16)
    grad_up = (grad_hidden * gate * sig).astype(jnp.bfloat16)
    grad_weight = lax.dot_general(
        lax.all_gather(hidden, "fsdp", axis=0, tiled=True),
        spread,
        (((0,), (0,)), ((), ())),
        preferred_element_type=jnp.float32,
    )
    return (grad_gate, grad_up, grad_weight.astype(jnp.bfloat16))


def solution(mesh):
    placed = (P("fsdp", "tensor"), P("fsdp", "tensor"), P("fsdp", "tensor"), P("tensor", "fsdp"))
    return jax.shard_map(
        shards,
        mesh=mesh,
        in_specs=placed,
        out_specs=(P("fsdp", "tensor"), P("fsdp", "tensor"), P("tensor", "fsdp")),
        check_vma=False,
    )
```

profile of v0, /device:TPU:32, one launch (start us, length us, event | category | flops | bytes accessed | tf_op | source)
XLA Modules:
  0.0 550.4 jit_solution(6163505027993967930)
XLA Ops:
  7.2 0.0 copy-start
  7.2 0.0 all-reduce.2.cloned.1.call-start
  7.2 21.7 %all_gather.6 = bf16[16,16384]{1,0:T(8,128)(2,1)S(1)} all-gather(bf16[16,1024]{1,0:T(8,128)(2,1)} %param.4), channel_id=1, replica_groups=mesh['fsdp'=32,'tensor'=16] {'tensor'}, dimensions={1}, use_global_device_ids=true | all-gather | bytes 557056 | tf_op jit(solution)/shard_map/all_gather | solution.py:8
  29.0 49.1 %all_to_all.19 = bf16[16,32,512]{2,0,1:T(8,128)(2,1)S(1)} all-to-all(bf16[16,32,512]{2,0,1:T(8,128)(2,1)S(1)} %bitcast.13), channel_id=1, replica_groups=mesh['fsdp'=32,'tensor'=16] {'fsdp'}, dimensions={1} | all-to-all | bytes 1048576 | tf_op jit(solution)/shard_map/all_to_all | solution.py:9
  78.0 0.0 copy-done
  78.0 2.9 fusion.10
  81.0 0.0 copy-start.1
  81.0 0.0 copy-start.2
  81.0 0.0 all-reduce.2.cloned.1.call-update
  81.0 0.0 all-gather.2.cloned.1.call-start
  81.1 311.7 %all-reduce.2.cloned.1.call-done = f32[512,1664]{1,0:T(8,128)} async-done(((f32[512,1664]{1,0:T(8,128)}), f32[512,1664]{1,0:T(8,128)}) %all-reduce.2.cloned.1.call-update) | async-done | bytes 3407888 | tf_op jit(solution)/shard_map/psum | solution.py:16
  392.8 0.0 copy-done.1
  392.8 0.0 copy-done.2
  392.8 1.6 fusion.9
  394.4 0.0 all-gather.2.cloned.1.call-update
  394.4 145.4 %all-gather.2.cloned.1.call-done = bf16[512,1664]{1,0:T(8,128)(2,1)} async-done(((bf16[16,1664]{1,0:T(8,128)(2,1)}), bf16[512,1664]{1,0:T(8,128)(2,1)}) %all-gather.2.cloned.1.call-update) | async-done | bytes 1703952 | tf_op jit(solution)/shard_map/all_gather | solution.py:23
  539.8 3.7 convolution_convert_fusion
  (1 shorter events, 0.0 us)
Async XLA Ops:
  7.2 70.9 %copy-start = (bf16[1664,512]{1,0:T(8,128)(2,1)S(1)}, bf16[1664,512]{1,0:T(8,128)(2,1)}, u32[]{:S(2)}) copy-start(bf16[1664,512]{1,0:T(8,128)(2,1)} %param.7) | copy-start | bytes 5111812
  7.2 385.6 %all-reduce.2.cloned.1.call-start = ((), (), s32[]{:S(2)}) async-start(), calls=%async_computation.1 | async-start | bytes 6815744 | tf_op jit(solution)/shard_map/psum | solution.py:16
  81.0 311.8 %copy-start.1 = (bf16[16,1664]{1,0:T(8,128)(2,1)S(1)}, bf16[16,1664]{1,0:T(8,128)(2,1)}, u32[]{:S(2)}) copy-start(bf16[16,1664]{1,0:T(8,128)(2,1)} %param.5) | copy-start | bytes 159748
  81.0 311.8 %copy-start.2 = (bf16[16,1664]{1,0:T(8,128)(2,1)S(1)}, bf16[16,1664]{1,0:T(8,128)(2,1)}, u32[]{:S(2)}) copy-start(bf16[16,1664]{1,0:T(8,128)(2,1)} %param.6) | copy-start | bytes 159748
  81.0 458.8 %all-gather.2.cloned.1.call-start = ((), (), s32[]{:S(2)}) async-start(), calls=%async_computation.2 | async-start | bytes 1757184 | tf_op jit(solution)/shard_map/all_gather | solution.py:23
Sparse Core Ops, SparseCore 0:
  81.1 311.6 all-reduce.1
  397.0 142.8 all-gather.1
where the time goes:
time: 551 us; the launch traced here: 550 us
  waiting for transfers between devices  457 us (83%)
  blocking collectives  70.8 us (13%)
  between operations  14.1 us (3%)
  matrix products  6.65 us (1%)
    psum x1, waiting for transfers between devices, shards(): summed = lax.psum(partial_all, 'fsdp')  312 us
    all_gather x1, waiting for transfers between devices, shards(): lax.all_gather(hidden, 'fsdp', axis=0, tiled=True)  145 us
    all_to_all x1, blocking collectives, shards(): lax.all_to_all(full_rows, 'fsdp', split_axis=1, concat_axis=0, tiled=True)  49.1 us
    all_gather x1, blocking collectives, shards(): full_rows = lax.all_gather(grad_out, 'tensor', axis=1, tiled=True)  21.7 us
  transfers between devices with their start and end apart: 2, of which 2 were waited for; matrix products, arithmetic and copies ran while one was open for 0% of the time, Pallas kernels for 0%

commit v1 on v0

v1 whole, which is shorter than its diff:
```python
import functools

import jax
import jax.numpy as jnp
from jax import lax
from jax.experimental import pallas as pl
from jax.experimental.pallas import tpu as pltpu
from jax.sharding import PartitionSpec as P

MESH = pl.DeviceIdType.MESH
F32, BF16 = jnp.float32, jnp.bfloat16
NZ, NX, NY = 16, 2, 4
FWD, BWD = 8, 7
COLS = ((0, 896), (896, 768))


def wrap(z):
    return lax.rem(z + 2 * NZ, NZ)


def kernel(
    g_ref, gate_ref, up_ref, w_hbm, gg_ref, gu_ref, gw_hbm,
    w_ref, hid, spread, part0, part1, fa, fb, gw_ref,
    rf0, rf1, rb0, rb1, sf0, sf1, sb0, sb1, xs0, xs1, xr0, xr1,
    ag_s, ag_r, rs_s, rs_r, hx_s, hx_r, px_s, px_r, pl_s, pl_r, co_s, co_r, fx_s, fx_r, loc,
):
    f, t = lax.axis_index("fsdp"), lax.axis_index("tensor")
    z, xh = f // 2, lax.rem(f, 2)
    xl, y, core = t // (2 * NY), lax.rem(t // 2, NY), lax.rem(t, 2)
    part, rf, rb, sf, sb = (part0, part1), (rf0, rf1), (rb0, rb1), (sf0, sf1), (sb0, sb1)
    xsend, xrecv = (xs0, xs1), (xr0, xr1)

    up_z = (2 * wrap(z + 1) + xh, t)
    down_z = (2 * wrap(z - 1) + xh, t)
    x_peer = (2 * z + 1 - xh, t)
    core_peer = (f, t + 1 - 2 * core)
    plane = [(dx, dy) for dx in range(NX) for dy in range(NY) if (dx, dy) != (0, 0)]

    def chip(dx, dy):
        return lax.rem(xl + dx, NX) * 2 * NY + lax.rem(y + dy, NY) * 2

    def rows16(i):
        return pl.ds(pl.multiple_of(16 * i, 16), 16)

    def rows32(i):
        return pl.ds(pl.multiple_of(32 * i, 32), 32)

    def remote(src, dst, ss, rs, dev):
        return pltpu.make_async_remote_copy(
            src_ref=src, dst_ref=dst, send_sem=ss, recv_sem=rs, device_id=dev, device_id_type=MESH
        )

    own_diag = t == z

    bar = pltpu.get_barrier_semaphore()
    for dev in [up_z, down_z, x_peer, core_peer] + [(f, chip(dx, dy) + core) for dx, dy in plane]:
        pl.semaphore_signal(bar, inc=1, device_id=dev, device_id_type=MESH)
    for h in range(2):
        @pl.when(jnp.logical_not(own_diag & (xh == h)))
        def _():
            pl.semaphore_signal(bar, inc=1, device_id=(2 * t + h, z), device_id_type=MESH)

    w_copy = pltpu.make_async_copy(w_hbm, w_ref, loc.at[0])
    w_copy.start()

    gate, up = gate_ref[...].astype(F32), up_ref[...].astype(F32)
    sig = jax.nn.sigmoid(gate)
    hid[rows16(f), :] = (gate * sig * up).astype(BF16)
    fa[...] = up * sig * (1.0 + gate * (1.0 - sig))
    fb[...] = gate * sig

    @pl.when(own_diag)
    def _():
        pl.semaphore_wait(bar, 4 + len(plane) + 1)

    @pl.when(jnp.logical_not(own_diag))
    def _():
        pl.semaphore_wait(bar, 4 + len(plane) + 2)

    pending = []

    def perm(h):
        return remote(g_ref.at[:, pl.ds(512 * h, 512)], spread.at[rows16(f)], px_s.at[h], px_r.at[xh], (2 * t + h, z))

    for h in range(2):
        mine = own_diag & (xh == h)

        @pl.when(mine)
        def _():
            pltpu.make_async_copy(g_ref.at[:, pl.ds(512 * h, 512)], spread.at[rows16(f)], loc.at[1]).start()

        @pl.when(jnp.logical_not(mine))
        def _():
            perm(h).start()

    def ag_copy(way, s, b):
        origin = wrap(z - (s - 1)) if way == 0 else wrap(z + (s - 1))
        rows = rows16(2 * origin + (xh if b == 0 else 1 - xh))
        k = (way * 2 + b) * FWD + s - 1
        return remote(hid.at[rows], hid.at[rows], ag_s.at[k], ag_r.at[k], up_z if way == 0 else down_z)

    def ag_recv(way, s, b):
        origin = wrap(z - s) if way == 0 else wrap(z + s)
        rows = rows16(2 * origin + (xh if b == 0 else 1 - xh))
        k = (way * 2 + b) * FWD + s - 1
        remote(hid.at[rows], hid.at[rows], ag_s.at[k], ag_r.at[k], up_z if way == 0 else down_z).wait_recv()

    def hops(way):
        return FWD if way == 0 else BWD

    def ag_step(s):
        for b in range(2):
            for way in range(2):
                if s > 1 and s - 1 <= hops(way):
                    ag_recv(way, s - 1, b)
                if s <= hops(way):
                    c = ag_copy(way, s, b)
                    c.start()
                    pending.append(c)
            if s == 1 and b == 0:
                c = remote(hid.at[rows16(f)], hid.at[rows16(f)], hx_s, hx_r, x_peer)
                c.start()
                pending.append(c)
                other = rows16(2 * z + 1 - xh)
                remote(hid.at[other], hid.at[other], hx_s, hx_r, x_peer).wait_recv()

    ag_step(1)

    for j in range(2):
        mine = own_diag & (xh == j)
        rows = rows16(2 * t + j)

        @pl.when(mine)
        def _():
            pltpu.make_async_copy(g_ref.at[:, pl.ds(512 * j, 512)], spread.at[rows], loc.at[1]).wait()

        @pl.when(jnp.logical_not(mine))
        def _():
            remote(g_ref.at[:, pl.ds(512 * j, 512)], spread.at[rows], px_s.at[j], px_r.at[j], (2 * t + j, z)).wait_recv()

    for r, (dx, dy) in enumerate(plane):
        c = remote(spread.at[rows32(t)], spread.at[rows32(t)], pl_s.at[r], pl_r.at[r], (f, chip(dx, dy) + core))
        c.start()
        pending.append(c)
    c = remote(spread.at[rows32(t)], spread.at[rows32(t)], co_s.at[7], co_r.at[7], core_peer)
    c.start()
    pending.append(c)

    ag_step(2)

    for r, (dx, dy) in enumerate(plane):
        src = rows32(chip(NX - dx, NY - dy) + core)
        remote(spread.at[src], spread.at[src], pl_s.at[r], pl_r.at[r], core_peer).wait_recv()
        c = remote(spread.at[src], spread.at[src], co_s.at[r], co_r.at[r], core_peer)
        c.start()
        pending.append(c)
    ag_step(3)
    for r, (dx, dy) in enumerate(plane + [(0, 0)]):
        src = rows32(chip(NX - dx, NY - dy) + 1 - core)
        remote(spread.at[src], spread.at[src], co_s.at[r], co_r.at[r], core_peer).wait_recv()
    w_copy.wait()

    def matmul(c):
        start, width = COLS[c]
        for i in range(0, width, 256):
            n = min(256, width - i)
            part[c][:, i : i + n] = lax.dot_general(
                spread[...], w_ref[start + i : start + i + n, :], (((1,), (1,)), ((), ())), preferred_element_type=F32
            )

    def rs_target(way, s):
        return wrap(z + FWD + 1 - s) if way == 0 else wrap(z - (BWD + 1 - s))

    def rs_step(s, c):
        for way in range(2):
            if s > hops(way):
                continue
            out = (sf, sb)[way][c].at[s - 1]
            inn = (rf, rb)[way][c]
            total = part[c][rows32(rs_target(way, s)), :]
            if s > 1:
                rs_recv(way, s - 1, c)
                total = total + inn[s - 2].astype(F32)
            out[...] = total.astype(BF16)
            k = (way * 2 + c) * FWD + s - 1
            cp = remote(out, inn.at[s - 1], rs_s.at[k], rs_r.at[k], up_z if way == 0 else down_z)
            cp.start()
            pending.append(cp)

    def rs_recv(way, s, c):
        inn = (rf, rb)[way][c]
        k = (way * 2 + c) * FWD + s - 1
        remote(inn.at[s - 1], inn.at[s - 1], rs_s.at[k], rs_r.at[k], up_z if way == 0 else down_z).wait_recv()

    def gw_tile(i, n):
        gw_ref[i : i + n, :] = lax.dot_general(
            hid[:, i : i + n], spread[...], (((0,), (0,)), ((), ())), preferred_element_type=F32
        ).astype(BF16)
        cp = pltpu.make_async_copy(gw_ref.at[pl.ds(i, n)], gw_hbm.at[pl.ds(i, n)], loc.at[2 + i // 256])
        cp.start()
        out_copies.append(cp)

    out_copies = []
    for c in range(2):
        matmul(c)
        rs_step(1, c)
    ag_step(4)
    tiles = [(i, min(256, 1664 - i)) for i in range(0, 1664, 256)]
    for s in range(2, FWD + 1):
        for c in range(2):
            rs_step(s, c)
        if s + 3 <= FWD + 1:
            ag_step(s + 3)
        else:
            for _ in range(3):
                if tiles:
                    gw_tile(*tiles.pop(0))

    for tile in tiles:
        gw_tile(*tile)

    keep = []
    for c in range(2):
        rs_recv(0, FWD, c)
        rs_recv(1, BWD, c)

        def total(i):
            rows = pl.ds(pl.multiple_of(16 * i, 16), 16)
            return part[c][rows16(2 * z + i), :] + rf[c][FWD - 1, rows, :].astype(F32) + rb[c][BWD - 1, rows, :].astype(F32)

        xsend[c][...] = total(1 - xh).astype(BF16)
        cp = remote(xsend[c], xrecv[c], fx_s.at[c], fx_r.at[c], x_peer)
        cp.start()
        pending.append(cp)
        keep.append(total(xh))
    for c in range(2):
        start, width = COLS[c]
        remote(xsend[c], xrecv[c], fx_s.at[c], fx_r.at[c], x_peer).wait_recv()
        grad = keep[c] + xrecv[c][...].astype(F32)
        gg_ref[:, start : start + width] = (grad * fa[:, start : start + width]).astype(BF16)
        gu_ref[:, start : start + width] = (grad * fb[:, start : start + width]).astype(BF16)

    for cp in out_copies:
        cp.wait()
    for cp in pending:
        cp.wait_send()
    for h in range(2):
        @pl.when(jnp.logical_not(own_diag & (xh == h)))
        def _():
            perm(h).wait_send()


def shards(grad_out, gate_pre, up_pre, down_weight):
    tokens, hidden, model = NZ * 2 * gate_pre.shape[0], gate_pre.shape[1], down_weight.shape[1]
    dma = pltpu.SemaphoreType.DMA
    widths = [w for _, w in COLS]
    return pl.pallas_call(
        kernel,
        out_shape=(
            jax.ShapeDtypeStruct(gate_pre.shape, BF16),
            jax.ShapeDtypeStruct(up_pre.shape, BF16),
            jax.ShapeDtypeStruct(down_weight.shape, BF16),
        ),
        in_specs=[pl.BlockSpec(memory_space=pltpu.VMEM)] * 3 + [pl.BlockSpec(memory_space=pl.ANY)],
        out_specs=(
            pl.BlockSpec(memory_space=pltpu.VMEM),
            pl.BlockSpec(memory_space=pltpu.VMEM),
            pl.BlockSpec(memory_space=pl.ANY),
        ),
        scratch_shapes=[
            pltpu.VMEM((hidden, model), BF16),
            pltpu.VMEM((tokens, hidden), BF16),
            pltpu.VMEM((tokens, model), BF16),
            pltpu.VMEM((tokens, widths[0]), F32),
            pltpu.VMEM((tokens, widths[1]), F32),
            pltpu.VMEM(gate_pre.shape, F32),
            pltpu.VMEM(gate_pre.shape, F32),
            pltpu.VMEM((hidden, model), BF16),
        ]
        + [pltpu.VMEM((n, 32, w), BF16) for n in (FWD, BWD, FWD, BWD) for w in widths]
        + [pltpu.VMEM((16, w), BF16) for _ in range(2) for w in widths]
        + [
            dma((4 * FWD,)), dma((4 * FWD,)), dma((4 * FWD,)), dma((4 * FWD,)),
            dma, dma, dma((2,)), dma((2,)), dma((7,)), dma((7,)), dma((8,)), dma((8,)), dma((2,)), dma((2,)), dma((9,)),
        ],
        compiler_params=pltpu.CompilerParams(collective_id=0, has_side_effects=True, vmem_limit_bytes=40 * 2**20),
        cost_estimate=pl.CostEstimate(flops=4 * tokens * hidden * model, bytes_accessed=2**22, transcendentals=0),
    )(grad_out, gate_pre, up_pre, down_weight)


def solution(mesh):
    placed = (P("fsdp", "tensor"), P("fsdp", "tensor"), P("fsdp", "tensor"), P("tensor", "fsdp"))
    return jax.shard_map(
        shards,
        mesh=mesh,
        in_specs=placed,
        out_specs=(P("fsdp", "tensor"), P("fsdp", "tensor"), P("tensor", "fsdp")),
        check_vma=False,
    )
```

time: 551 us -> 77.4 us (0.14)
  waiting for transfers between devices: 457 us -> 0 us
  blocking collectives: 70.8 us -> 0 us
  Pallas kernels: 0 us -> 70.1 us
  between operations: 14.1 us -> 0.65 us
  matrix products: 6.65 us -> 0 us
  local copies, waits for them, and re-layouts: 0.07 us -> 6.25 us
    psum x1 -> x0, waiting for transfers between devices: 312 us -> none  [shards(): summed = lax.psum(partial_all, 'fsdp')]
    all_gather x1 -> x0, waiting for transfers between devices: 145 us -> none  [shards(): lax.all_gather(hidden, 'fsdp', axis=0, tiled=True)]
    pallas_call x0 -> x1, Pallas kernels: none -> 70.1 us  [shards(): pl.pallas_call(kernel, out_shape=(jax.ShapeDtypeStruct(gate_pre.shape, BF...]
    all_to_all x1 -> x0, blocking collectives: 49.1 us -> none  [shards(): lax.all_to_all(full_rows, 'fsdp', split_axis=1, concat_axis=0, tiled=True)]
    all_gather x1 -> x0, blocking collectives: 21.7 us -> none  [shards(): full_rows = lax.all_gather(grad_out, 'tensor', axis=1, tiled=True)]
    dot_general x2 -> x0, matrix products: 6.65 us -> none  [the longest x1 3.72 us: shards(): lax.dot_general(lax.all_gather(hidden, 'fsdp', axis=0, tiled=True), sprea...]
    unnamed x6 -> x11, local copies, waits for them, and re-layouts: 0.02 us -> 6.25 us
  transfers between devices with their start and end apart: 2 -> 0, of which waited for: 2 -> 0; matrix products, arithmetic and copies ran while one was open for 0% -> 0% of each run, Pallas kernels for 0% -> 0%
where the time goes in v1:
time: 77.4 us; the launch traced here: 77 us
  Pallas kernels  70.1 us (91%)
  local copies, waits for them, and re-layouts  6.25 us (8%)
    pallas_call x1, Pallas kernels, shards(): pl.pallas_call(kernel, out_shape=(jax.ShapeDtypeStruct(gate_pre.shape, BF...  70.1 us
    unnamed x11, local copies, waits for them, and re-layouts  6.25 us

profile of v1, /device:TPU:32, one launch (start us, length us, event | category | flops | bytes accessed | tf_op | source)
XLA Modules:
  0.0 77.0 jit_solution(5937190521689917507)
XLA Ops:
  0.6 0.0 copy-start
  0.6 1.4 %copy-done = bf16[1664,512]{1,0:T(8,128)(2,1)S(1)} copy-done((bf16[1664,512]{1,0:T(8,128)(2,1)S(1)}, bf16[1664,512]{1,0:T(8,128)(2,1)}, u32[]{:S(2)}) %copy-start) | copy-done | bytes 1703960
  2.1 0.0 copy-start.1
  2.1 0.8 %copy-done.1 = bf16[16,1664]{1,0:T(8,128)(2,1)S(1)} copy-done((bf16[16,1664]{1,0:T(8,128)(2,1)S(1)}, bf16[16,1664]{1,0:T(8,128)(2,1)}, u32[]{:S(2)}) %copy-start.1) | copy-done | bytes 53272
  2.9 0.0 copy-start.2
  2.9 0.8 %copy-done.2 = bf16[16,1664]{1,0:T(8,128)(2,1)S(1)} copy-done((bf16[16,1664]{1,0:T(8,128)(2,1)S(1)}, bf16[16,1664]{1,0:T(8,128)(2,1)}, u32[]{:S(2)}) %copy-start.2) | copy-done | bytes 53272
  3.7 0.0 copy-start.3
  3.7 0.8 copy-done.3
  4.5 70.1 %shard_map.67 = (bf16[16,1664]{1,0:T(8,128)(2,1)S(1)}, bf16[16,1664]{1,0:T(8,128)(2,1)S(1)}, bf16[1664,512]{1,0:T(8,128)(2,1)S(1)}) custom-call(bf16[16,1024]{1,0:T(8,128)(2,1)S(1)} %copy-done.3, bf16[16,1664]{1,0:T(8,128)(2,1)S(1)} %copy-done.1, bf16[16,1664]{1,0:T(8,128)(2,1)S(1)} %copy-done.2, bf16[1664,512]{1,0:T(8,128)(2,1)S(1)} %copy-done), custom_call_target="tpu_custom_call" | custom-call | flops 1744830464 | bytes 4194304 | tf_op jit(solution)/shard_map/pallas_call | solution.py:257
  74.6 0.6 copy.10
  75.2 0.6 copy.11
  75.8 1.2 %copy.12 = bf16[1664,512]{1,0:T(8,128)(2,1)} copy(bf16[1664,512]{1,0:T(8,128)(2,1)S(1)} %get-tuple-element.8) | data formatting | bytes 3407872
Async XLA Ops:
  0.6 1.5 %copy-start = (bf16[1664,512]{1,0:T(8,128)(2,1)S(1)}, bf16[1664,512]{1,0:T(8,128)(2,1)}, u32[]{:S(2)}) copy-start(bf16[1664,512]{1,0:T(8,128)(2,1)} %w_hbm.1) | copy-start | bytes 5111812
  2.1 0.8 %copy-start.1 = (bf16[16,1664]{1,0:T(8,128)(2,1)S(1)}, bf16[16,1664]{1,0:T(8,128)(2,1)}, u32[]{:S(2)}) copy-start(bf16[16,1664]{1,0:T(8,128)(2,1)} %gate_ref.1) | copy-start | bytes 159748
  2.9 0.8 %copy-start.2 = (bf16[16,1664]{1,0:T(8,128)(2,1)S(1)}, bf16[16,1664]{1,0:T(8,128)(2,1)}, u32[]{:S(2)}) copy-start(bf16[16,1664]{1,0:T(8,128)(2,1)} %up_ref.1) | copy-start | bytes 159748
  3.7 0.8 copy-start.3

commit v2 on v1

v2 whole, which is shorter than its diff:
```python
import functools

import jax
import jax.numpy as jnp
from jax import lax
from jax.experimental import pallas as pl
from jax.experimental.pallas import tpu as pltpu
from jax.sharding import PartitionSpec as P

MESH = pl.DeviceIdType.MESH
F32, BF16 = jnp.float32, jnp.bfloat16
NZ, NX, NY = 16, 2, 4
FWD, BWD = 8, 7
CHUNKS = ((0, 384, False), (384, 384, False), (768, 896, True))
TREE = (
    ((0, 8, 7), (0, 3, 2), (1, 7, 6), (1, 2, 1)),
    ((0, 7, 6), (0, 2, 1), (1, 6, 5), (1, 1, 0)),
    ((0, 6, 5), (0, 1, 0), (1, 5, 4)),
    ((0, 5, 4), (1, 4, 3)),
    ((0, 4, 0), (1, 3, 0)),
)
SLOTS = [(way, o) for stage in TREE for way, o, _ in stage]
CROSS = SLOTS + [(0, 0)]
CUTS = (0, len(TREE[0]), len(TREE[0]) + len(TREE[1]), len(CROSS))


def wrap(z):
    return lax.rem(z + 2 * NZ, NZ)


def kernel(
    g_hbm, gate_hbm, up_hbm, w_hbm, gg_ref, gu_ref, gw_hbm,
    g_ref, gate_ref, up_ref, w_ref, hid, spread, fa, fb, gw_ref,
    part0, part1, part2, ts0, ts1, ts2, tr0, tr1, tr2, fs0, fs1, fr0, fr1, xsend, xrecv,
    ag_s, ag_r, t_s, t_r, fx_s, fx_r, x_s, x_r, hx_s, hx_r, px_s, px_r, pl_s, pl_r, co_s, co_r, loc,
):
    f, t = lax.axis_index("fsdp"), lax.axis_index("tensor")
    z, xh = f // 2, lax.rem(f, 2)
    xl, y, core = t // (2 * NY), lax.rem(t // 2, NY), lax.rem(t, 2)
    part, tsend, trecv = (part0, part1, part2), (ts0, ts1, ts2), (tr0, tr1, tr2)
    fsend, frecv = (fs0, fs1), (fr0, fr1)

    loads = [
        pltpu.make_async_copy(src, dst, loc.at[i])
        for i, (src, dst) in enumerate(((gate_hbm, gate_ref), (up_hbm, up_ref), (g_hbm, g_ref), (w_hbm, w_ref)))
    ]
    for cp in loads:
        cp.start()

    def along(d):
        return (2 * wrap(z + d) + xh, t)

    up_z = (2 * wrap(z + 1) + xh, t)
    down_z = (2 * wrap(z - 1) + xh, t)
    x_peer = (2 * z + 1 - xh, t)
    core_peer = (f, t + 1 - 2 * core)
    plane = [(dx, dy) for dx in range(NX) for dy in range(NY) if (dx, dy) != (0, 0)]

    def chip(dx, dy):
        return lax.rem(xl + dx, NX) * 2 * NY + lax.rem(y + dy, NY) * 2

    def rows16(i):
        return pl.ds(pl.multiple_of(16 * i, 16), 16)

    def rows32(i):
        return pl.ds(pl.multiple_of(32 * i, 32), 32)

    def remote(src, dst, ss, rs, dev):
        return pltpu.make_async_remote_copy(
            src_ref=src, dst_ref=dst, send_sem=ss, recv_sem=rs, device_id=dev, device_id_type=MESH
        )

    own_diag = t == z

    bar = pltpu.get_barrier_semaphore()
    reach = sorted({o - p if way == 0 else p - o for stage in TREE for way, o, p in stage} | {1, -1})
    reach = sorted(set(reach) | {-d for d in reach})
    for dev in [along(d) for d in reach] + [x_peer, core_peer] + [(f, chip(dx, dy) + core) for dx, dy in plane]:
        pl.semaphore_signal(bar, inc=1, device_id=dev, device_id_type=MESH)
    for h in range(2):
        @pl.when(jnp.logical_not(own_diag & (xh == h)))
        def _():
            pl.semaphore_signal(bar, inc=1, device_id=(2 * t + h, z), device_id_type=MESH)

    loads[0].wait()
    loads[1].wait()
    gate, up = gate_ref[...].astype(F32), up_ref[...].astype(F32)
    sig = jax.nn.sigmoid(gate)
    hid[rows16(f), :] = (gate * sig * up).astype(BF16)
    fa[...] = up * sig * (1.0 + gate * (1.0 - sig))
    fb[...] = gate * sig

    @pl.when(own_diag)
    def _():
        pl.semaphore_wait(bar, len(reach) + 2 + len(plane) + 1)

    @pl.when(jnp.logical_not(own_diag))
    def _():
        pl.semaphore_wait(bar, len(reach) + 2 + len(plane) + 2)

    pending = []
    loads[2].wait()

    def perm(h):
        return remote(g_ref.at[:, pl.ds(512 * h, 512)], spread.at[rows16(f)], px_s.at[h], px_r.at[xh], (2 * t + h, z))

    for h in range(2):
        mine = own_diag & (xh == h)

        @pl.when(mine)
        def _():
            pltpu.make_async_copy(g_ref.at[:, pl.ds(512 * h, 512)], spread.at[rows16(f)], loc.at[4]).start()

        @pl.when(jnp.logical_not(mine))
        def _():
            perm(h).start()

    def ag_copy(way, s):
        rows = rows16(2 * (wrap(z - (s - 1)) if way == 0 else wrap(z + (s - 1))) + xh)
        k = way * FWD + s - 1
        return remote(hid.at[rows], hid.at[rows], ag_s.at[k], ag_r.at[k], up_z if way == 0 else down_z)

    def ag_arrived(way, s):
        rows = rows16(2 * (wrap(z - s) if way == 0 else wrap(z + s)) + xh)
        k = way * FWD + s - 1
        remote(hid.at[rows], hid.at[rows], ag_s.at[k], ag_r.at[k], up_z if way == 0 else down_z).wait_recv()

    def hid_x(way, s, h):
        rows = rows16(2 * (wrap(z - s) if way == 0 else wrap(z + s)) + h)
        k = way * FWD + s
        return remote(hid.at[rows], hid.at[rows], hx_s.at[k], hx_r.at[k], x_peer)

    def hops(way):
        return FWD if way == 0 else BWD

    def ag_step(s):
        for way in range(2):
            came = s - 1 <= hops(way) and (s > 1 or way == 0)
            if s > 1 and came:
                ag_arrived(way, s - 1)
            if s <= hops(way):
                c = ag_copy(way, s)
                c.start()
                pending.append(c)
            if came:
                c = hid_x(way, s - 1, xh)
                c.start()
                pending.append(c)

    ag_step(1)
    ag_step(2)

    for j in range(2):
        mine = own_diag & (xh == j)
        rows = rows16(2 * t + j)

        @pl.when(mine)
        def _():
            pltpu.make_async_copy(g_ref.at[:, pl.ds(512 * j, 512)], spread.at[rows], loc.at[4]).wait()

        @pl.when(jnp.logical_not(mine))
        def _():
            remote(g_ref.at[:, pl.ds(512 * j, 512)], spread.at[rows], px_s.at[j], px_r.at[j], (2 * t + j, z)).wait_recv()

    for r, (dx, dy) in enumerate(plane):
        c = remote(spread.at[rows32(t)], spread.at[rows32(t)], pl_s.at[r], pl_r.at[r], (f, chip(dx, dy) + core))
        c.start()
        pending.append(c)
    c = remote(spread.at[rows32(t)], spread.at[rows32(t)], co_s.at[7], co_r.at[7], core_peer)
    c.start()
    pending.append(c)

    ag_step(3)

    for r, (dx, dy) in enumerate(plane):
        src = rows32(chip(NX - dx, NY - dy) + core)
        remote(spread.at[src], spread.at[src], pl_s.at[r], pl_r.at[r], core_peer).wait_recv()
        c = remote(spread.at[src], spread.at[src], co_s.at[r], co_r.at[r], core_peer)
        c.start()
        pending.append(c)
    ag_step(4)
    for r, (dx, dy) in enumerate(plane + [(0, 0)]):
        src = rows32(chip(NX - dx, NY - dy) + 1 - core)
        remote(spread.at[src], spread.at[src], co_s.at[r], co_r.at[r], core_peer).wait_recv()
    loads[3].wait()

    def matmul(c):
        start, width, _ = CHUNKS[c]
        for i in range(0, width, 256):
            n = min(256, width - i)
            part[c][:, i : i + n] = lax.dot_general(
                spread[...], w_ref[start + i : start + i + n, :], (((1,), (1,)), ((), ())), preferred_element_type=F32
            )

    def dest(way, o):
        return wrap(z + o) if way == 0 else wrap(z - o)

    def hop(c, way, o, p):
        i, d = SLOTS.index((way, o)), o - p if way == 0 else p - o
        return remote(tsend[c].at[i], trecv[c].at[i], t_s.at[c, i], t_r.at[c, i], along(d))

    def cross(g):
        at = pl.ds(CUTS[g], CUTS[g + 1] - CUTS[g])
        return remote(xsend.at[at], xrecv.at[at], x_s.at[g], x_r.at[g], x_peer)

    def cross_x(c):
        for g in range(3):
            for i in range(CUTS[g], CUTS[g + 1]):
                xsend[i] = part[c][rows16(2 * dest(*CROSS[i]) + 1 - xh), :].astype(BF16)
            cross(g).start()
            pending.append(cross(g))

    def gathered(c, way, o):
        if CHUNKS[c][2]:
            total = part[c][rows16(2 * dest(way, o) + xh), :] + xrecv[CROSS.index((way, o))].astype(F32)
        else:
            total = part[c][rows32(dest(way, o)), :]
        for stage in TREE:
            for w, k, p in stage:
                if p == o and (w == way or o == 0):
                    hop(c, w, k, p).wait_recv()
                    total = total + trecv[c][SLOTS.index((w, k))].astype(F32)
        return total

    def tree_stage(n, c):
        if CHUNKS[c][2] and n < 3:
            cross(n).wait_recv()
        for way, o, p in TREE[n]:
            tsend[c][SLOTS.index((way, o))] = gathered(c, way, o).astype(BF16)
            cp = hop(c, way, o, p)
            cp.start()
            pending.append(cp)

    def gw_tile(i, n):
        gw_ref[i : i + n, :] = lax.dot_general(
            hid[:, i : i + n], spread[...], (((0,), (0,)), ((), ())), preferred_element_type=F32
        ).astype(BF16)
        cp = pltpu.make_async_copy(gw_ref.at[pl.ds(i, n)], gw_hbm.at[pl.ds(i, n)], loc.at[5 + i // 256])
        cp.start()
        out_copies.append(cp)

    out_copies = []
    matmul(2)
    cross_x(2)
    for c in range(2):
        matmul(c)
        tree_stage(0, c)
    ag_step(5)
    for n in range(1, len(TREE)):
        for c in range(2):
            tree_stage(n, c)
        tree_stage(n - 1, 2)
        if n + 5 <= FWD + 1:
            ag_step(n + 5)
    tree_stage(len(TREE) - 1, 2)
    for n in range(len(TREE) + 5, FWD + 2):
        ag_step(n)
    for way in range(2):
        for n in range(0 if way == 0 else 1, hops(way) + 1):
            hid_x(way, n, 1 - xh).wait_recv()
    for i in range(0, 1664, 256):
        gw_tile(i, min(256, 1664 - i))

    def final(c):
        return remote(fsend[c].at[1 - xh], frecv[c], fx_s.at[c], fx_r.at[c], x_peer)

    def gradients(c, grad):
        cols = pl.ds(CHUNKS[c][0], CHUNKS[c][1])
        gg_ref[:, cols] = (grad * fa[:, cols]).astype(BF16)
        gu_ref[:, cols] = (grad * fb[:, cols]).astype(BF16)

    for c in range(2):
        total = gathered(c, 0, 0)
        fsend[c][0], fsend[c][1] = total[:16], total[16:]
        final(c).start()
        pending.append(final(c))
    for c in range(2):
        final(c).wait_recv()
        grad = fsend[c][xh] + frecv[c][...]
        gradients(c, grad)
    gradients(2, gathered(2, 0, 0))

    for cp in out_copies:
        cp.wait()
    for cp in pending:
        cp.wait_send()
    for h in range(2):
        @pl.when(jnp.logical_not(own_diag & (xh == h)))
        def _():
            perm(h).wait_send()


def shards(grad_out, gate_pre, up_pre, down_weight):
    tokens, hidden, model = NZ * 2 * gate_pre.shape[0], gate_pre.shape[1], down_weight.shape[1]
    dma = pltpu.SemaphoreType.DMA
    widths = [w for _, w, _ in CHUNKS]
    heights = [16 if x_first else 32 for _, _, x_first in CHUNKS]
    return pl.pallas_call(
        kernel,
        out_shape=(
            jax.ShapeDtypeStruct(gate_pre.shape, BF16),
            jax.ShapeDtypeStruct(up_pre.shape, BF16),
            jax.ShapeDtypeStruct(down_weight.shape, BF16),
        ),
        in_specs=[pl.BlockSpec(memory_space=pltpu.HBM)] * 4,
        out_specs=(
            pl.BlockSpec(memory_space=pltpu.VMEM),
            pl.BlockSpec(memory_space=pltpu.VMEM),
            pl.BlockSpec(memory_space=pl.ANY),
        ),
        scratch_shapes=[
            pltpu.VMEM(grad_out.shape, BF16),
            pltpu.VMEM(gate_pre.shape, BF16),
            pltpu.VMEM(up_pre.shape, BF16),
            pltpu.VMEM((hidden, model), BF16),
            pltpu.VMEM((tokens, hidden), BF16),
            pltpu.VMEM((tokens, model), BF16),
            pltpu.VMEM(gate_pre.shape, F32),
            pltpu.VMEM(gate_pre.shape, F32),
            pltpu.VMEM((hidden, model), BF16),
        ]
        + [pltpu.VMEM((tokens, w), F32) for w in widths]
        + [pltpu.VMEM((15, h, w), BF16) for _ in range(2) for h, w in zip(heights, widths)]
        + [pltpu.VMEM((2, 16, w), F32) for w in widths[:2]]
        + [pltpu.VMEM((16, w), F32) for w in widths[:2]]
        + [pltpu.VMEM((16, 16, widths[2]), BF16)] * 2
        + [
            dma((2 * FWD,)), dma((2 * FWD,)), dma((3, 15)), dma((3, 15)), dma((2,)), dma((2,)), dma((3,)), dma((3,)),
            dma((2 * FWD,)), dma((2 * FWD,)), dma((2,)), dma((2,)), dma((7,)), dma((7,)), dma((8,)), dma((8,)), dma((12,)),
        ],
        compiler_params=pltpu.CompilerParams(collective_id=0, has_side_effects=True, vmem_limit_bytes=40 * 2**20),
        cost_estimate=pl.CostEstimate(flops=4 * tokens * hidden * model, bytes_accessed=2**22, transcendentals=0),
    )(grad_out, gate_pre, up_pre, down_weight)


def solution(mesh):
    placed = (P("fsdp", "tensor"), P("fsdp", "tensor"), P("fsdp", "tensor"), P("tensor", "fsdp"))
    return jax.shard_map(
        shards,
        mesh=mesh,
        in_specs=placed,
        out_specs=(P("fsdp", "tensor"), P("fsdp", "tensor"), P("tensor", "fsdp")),
        check_vma=False,
    )
```

time: 77.4 us -> 71.8 us (0.928)
  the two profiles are of different devices: /device:TPU:32 before, /device:TPU:10 now
where the time goes in v2:
time: 71.8 us; the launch traced here: 71.5 us
  Pallas kernels  64.6 us (90%)
  local copies, waits for them, and re-layouts  6.25 us (9%)
    pallas_call x1, Pallas kernels, shards(): pl.pallas_call(kernel, out_shape=(jax.ShapeDtypeStruct(gate_pre.shape, BF...  64.6 us
    unnamed x11, local copies, waits for them, and re-layouts  6.25 us

profile of v2, /device:TPU:10, one launch (start us, length us, event | category | flops | bytes accessed | tf_op | source)
XLA Modules:
  0.0 71.5 jit_solution(2330531229633307241)
XLA Ops:
  0.6 0.0 copy-start
  0.6 1.4 %copy-done = bf16[1664,512]{1,0:T(8,128)(2,1)S(1)} copy-done((bf16[1664,512]{1,0:T(8,128)(2,1)S(1)}, bf16[1664,512]{1,0:T(8,128)(2,1)}, u32[]{:S(2)}) %copy-start) | copy-done | bytes 1703960
  2.1 0.0 copy-start.1
  2.1 0.8 %copy-done.1 = bf16[16,1664]{1,0:T(8,128)(2,1)S(1)} copy-done((bf16[16,1664]{1,0:T(8,128)(2,1)S(1)}, bf16[16,1664]{1,0:T(8,128)(2,1)}, u32[]{:S(2)}) %copy-start.1) | copy-done | bytes 53272
  2.9 0.0 copy-start.2
  2.9 0.8 %copy-done.2 = bf16[16,1664]{1,0:T(8,128)(2,1)S(1)} copy-done((bf16[16,1664]{1,0:T(8,128)(2,1)S(1)}, bf16[16,1664]{1,0:T(8,128)(2,1)}, u32[]{:S(2)}) %copy-start.2) | copy-done | bytes 53272
  3.7 0.0 copy-start.3
  3.7 0.8 %copy-done.3 = bf16[16,1024]{1,0:T(8,128)(2,1)S(1)} copy-done((bf16[16,1024]{1,0:T(8,128)(2,1)S(1)}, bf16[16,1024]{1,0:T(8,128)(2,1)}, u32[]{:S(2)}) %copy-start.3) | copy-done | bytes 32792
  4.5 64.6 %shard_map.67 = (bf16[16,1664]{1,0:T(8,128)(2,1)S(1)}, bf16[16,1664]{1,0:T(8,128)(2,1)S(1)}, bf16[1664,512]{1,0:T(8,128)(2,1)S(1)}) custom-call(bf16[16,1024]{1,0:T(8,128)(2,1)S(1)} %copy-done.3, bf16[16,1664]{1,0:T(8,128)(2,1)S(1)} %copy-done.1, bf16[16,1664]{1,0:T(8,128)(2,1)S(1)} %copy-done.2, bf16[1664,512]{1,0:T(8,128)(2,1)S(1)} %copy-done), custom_call_target="tpu_custom_call" | custom-call | flops 1744830464 | bytes 4194304 | tf_op jit(solution)/shard_map/pallas_call | solution.py:298
  69.0 0.6 copy.10
  69.6 0.6 copy.11
  70.3 1.2 %copy.12 = bf16[1664,512]{1,0:T(8,128)(2,1)} copy(bf16[1664,512]{1,0:T(8,128)(2,1)S(1)} %get-tuple-element.8) | data formatting | bytes 3407872
Async XLA Ops:
  0.6 1.5 %copy-start = (bf16[1664,512]{1,0:T(8,128)(2,1)S(1)}, bf16[1664,512]{1,0:T(8,128)(2,1)}, u32[]{:S(2)}) copy-start(bf16[1664,512]{1,0:T(8,128)(2,1)} %w_hbm.1) | copy-start | bytes 5111812
  2.1 0.8 %copy-start.1 = (bf16[16,1664]{1,0:T(8,128)(2,1)S(1)}, bf16[16,1664]{1,0:T(8,128)(2,1)}, u32[]{:S(2)}) copy-start(bf16[16,1664]{1,0:T(8,128)(2,1)} %gate_hbm.1) | copy-start | bytes 159748
  2.9 0.8 %copy-start.2 = (bf16[16,1664]{1,0:T(8,128)(2,1)S(1)}, bf16[16,1664]{1,0:T(8,128)(2,1)}, u32[]{:S(2)}) copy-start(bf16[16,1664]{1,0:T(8,128)(2,1)} %up_hbm.1) | copy-start | bytes 159748
  3.7 0.8 %copy-start.3 = (bf16[16,1024]{1,0:T(8,128)(2,1)S(1)}, bf16[16,1024]{1,0:T(8,128)(2,1)}, u32[]{:S(2)}) copy-start(bf16[16,1024]{1,0:T(8,128)(2,1)} %g_hbm.1) | copy-start | bytes 98308

commit v3 on v2

--- a/solution.py
+++ b/solution.py
@@ -12,13 +12,7 @@
 NZ, NX, NY = 16, 2, 4
 FWD, BWD = 8, 7
 CHUNKS = ((0, 384, False), (384, 384, False), (768, 896, True))
-TREE = (
-    ((0, 8, 7), (0, 3, 2), (1, 7, 6), (1, 2, 1)),
-    ((0, 7, 6), (0, 2, 1), (1, 6, 5), (1, 1, 0)),
-    ((0, 6, 5), (0, 1, 0), (1, 5, 4)),
-    ((0, 5, 4), (1, 4, 3)),
-    ((0, 4, 0), (1, 3, 0)),
-)
+TREE = (((0, 8, 7), (0, 2, 1), (1, 7, 6), (1, 1, 0)), ((0, 7, 6), (0, 1, 0), (1, 6, 5)), ((0, 6, 5), (1, 5, 4)), ((0, 5, 4), (1, 4, 3)), ((0, 4, 3), (1, 3, 2)), ((0, 3, 0), (1, 2, 0)))
 SLOTS = [(way, o) for stage in TREE for way, o, _ in stage]
 CROSS = SLOTS + [(0, 0)]
 CUTS = (0, len(TREE[0]), len(TREE[0]) + len(TREE[1]), len(CROSS))
@@ -328,7 +322,7 @@
             dma((2 * FWD,)), dma((2 * FWD,)), dma((3, 15)), dma((3, 15)), dma((2,)), dma((2,)), dma((3,)), dma((3,)),
             dma((2 * FWD,)), dma((2 * FWD,)), dma((2,)), dma((2,)), dma((7,)), dma((7,)), dma((8,)), dma((8,)), dma((12,)),
         ],
-        compiler_params=pltpu.CompilerParams(collective_id=0, has_side_effects=True, vmem_limit_bytes=40 * 2**20),
+        compiler_params=pltpu.CompilerParams(collective_id=0, has_side_effects=True, vmem_limit_bytes=52 * 2**20),
         cost_estimate=pl.CostEstimate(flops=4 * tokens * hidden * model, bytes_accessed=2**22, transcendentals=0),
     )(grad_out, gate_pre, up_pre, down_weight)
 

time: 71.8 us -> 69.6 us (0.969)
  the two profiles are of different devices: /device:TPU:10 before, /device:TPU:16 now
where the time goes in v3:
time: 69.6 us; the launch traced here: 69.4 us
  Pallas kernels  63.9 us (92%)
  local copies, waits for them, and re-layouts  4.8 us (7%)
    pallas_call x1, Pallas kernels, shards(): pl.pallas_call(kernel, out_shape=(jax.ShapeDtypeStruct(gate_pre.shape, BF...  63.9 us
    unnamed x9, local copies, waits for them, and re-layouts  4.8 us

profile of v3, /device:TPU:16, one launch (start us, length us, event | category | flops | bytes accessed | tf_op | source)
XLA Modules:
  0.0 69.4 jit_solution(9312239731626906887)
XLA Ops:
  0.6 0.0 copy-start
  0.6 0.8 %copy-done = bf16[16,1664]{1,0:T(8,128)(2,1)S(1)} copy-done((bf16[16,1664]{1,0:T(8,128)(2,1)S(1)}, bf16[16,1664]{1,0:T(8,128)(2,1)}, u32[]{:S(2)}) %copy-start) | copy-done | bytes 53272
  1.4 0.0 copy-start.1
  1.4 0.8 %copy-done.1 = bf16[16,1664]{1,0:T(8,128)(2,1)S(1)} copy-done((bf16[16,1664]{1,0:T(8,128)(2,1)S(1)}, bf16[16,1664]{1,0:T(8,128)(2,1)}, u32[]{:S(2)}) %copy-start.1) | copy-done | bytes 53272
  2.3 0.0 copy-start.2
  2.3 0.8 %copy-done.2 = bf16[16,1024]{1,0:T(8,128)(2,1)S(1)} copy-done((bf16[16,1024]{1,0:T(8,128)(2,1)S(1)}, bf16[16,1024]{1,0:T(8,128)(2,1)}, u32[]{:S(2)}) %copy-start.2) | copy-done | bytes 32792
  3.0 63.9 %shard_map.67 = (bf16[16,1664]{1,0:T(8,128)(2,1)S(1)}, bf16[16,1664]{1,0:T(8,128)(2,1)S(1)}, bf16[1664,512]{1,0:T(8,128)(2,1)S(1)}) custom-call(bf16[16,1024]{1,0:T(8,128)(2,1)S(1)} %copy-done.2, bf16[16,1664]{1,0:T(8,128)(2,1)S(1)} %copy-done, bf16[16,1664]{1,0:T(8,128)(2,1)S(1)} %copy-done.1, bf16[1664,512]{1,0:T(8,128)(2,1)} %w_hbm.1), custom_call_target="tpu_custom_call" | custom-call | flops 1744830464 | bytes 4194304 | tf_op jit(solution)/shard_map/pallas_call | solution.py:292
  66.9 0.6 copy.10
  67.5 0.6 copy.11
  68.2 1.2 %copy.12 = bf16[1664,512]{1,0:T(8,128)(2,1)} copy(bf16[1664,512]{1,0:T(8,128)(2,1)S(1)} %get-tuple-element.8) | data formatting | bytes 3407872
Async XLA Ops:
  0.6 0.8 %copy-start = (bf16[16,1664]{1,0:T(8,128)(2,1)S(1)}, bf16[16,1664]{1,0:T(8,128)(2,1)}, u32[]{:S(2)}) copy-start(bf16[16,1664]{1,0:T(8,128)(2,1)} %gate_hbm.1) | copy-start | bytes 159748
  1.4 0.8 %copy-start.1 = (bf16[16,1664]{1,0:T(8,128)(2,1)S(1)}, bf16[16,1664]{1,0:T(8,128)(2,1)}, u32[]{:S(2)}) copy-start(bf16[16,1664]{1,0:T(8,128)(2,1)} %up_hbm.1) | copy-start | bytes 159748
  2.3 0.8 %copy-start.2 = (bf16[16,1024]{1,0:T(8,128)(2,1)S(1)}, bf16[16,1024]{1,0:T(8,128)(2,1)}, u32[]{:S(2)}) copy-start(bf16[16,1024]{1,0:T(8,128)(2,1)} %g_hbm.1) | copy-start | bytes 98308
